TPU v7x, 1024 devices: a whole 8x8x8 slice. The times are simulated.
1024 devices in a mesh: dp: 64 (over z, x), expert: 16 (over y, core).
Axes of the slice: x: 8, y: 8, z: 8, core: 2. Of those that a mesh axis runs over, the one named last changes fastest.
Arguments:
- d_out: bfloat16 [2, 131072, 2048], P(None, ('dp', 'expert')), may hold values from -6 to 6
- routes: int32 [2, 131072, 8], P(None, ('dp', 'expert')), may hold values from 0 to 127, as said below
- slots: int32 [2, 131072, 8], P(None, ('dp', 'expert')), may hold values from -1 to 15, as said below
- route_probs: bfloat16 [2, 131072, 8], P(None, ('dp', 'expert')), may hold values from 0.029907227 to 0.5
- token_counts: int32 [2, 1024], P(None, ('dp', 'expert')), may hold values from 42 to 128, as said below
- hidden: bfloat16 [2, 64, 256, 3072], P(None, 'dp', None, 'expert'), may hold values from -0.59765625 to 0.59765625
- w_down: bfloat16 [3072, 2048], P('expert'), may hold values from -0.21875 to 0.21875
Outputs:
- d_hidden: bfloat16 [2, 64, 256, 3072], P(None, 'dp', None, 'expert')
- d_w2: float32 [2048, 3072], P('dp', 'expert')
- d_probs: float32 [2, 131072, 8], P(None, ('dp', 'expert'))
Inputs may be any that keep to these rules, and one draw needn't show every extreme that they name: `routes`: each row names 8 different experts. Only experts below 4 belong to the window; window expert e is held by indices 4 * e to 4 * e + 3 of the expert axis, each with its share of the hidden units in order. A slot is -1 exactly where the route names an expert at or above 4 or where the token's position in its device's block of 128 is at or past that device's count; the routes of one device to one window expert in one microbatch hold distinct slots. In every microbatch one window expert receives 16 rows from every device. `token_counts`: A device's valid tokens are the first ones of its block.
All inputs are finite; a program needn't handle non-finite values.
Results may differ from a plain program's by a relative error of at most 0.003.
Values may be sent and summed in bfloat16 or wider, within the bound.
A program may use at most 32 MiB of HBM per device.

v0:
```python
import jax
import jax.numpy as jnp
from jax import lax
from jax.sharding import PartitionSpec as P

GROUP = 4


def expert_work(rows, weights, hidden_rows, weight, grad_scale):
    slot_count = rows.shape[0] * rows.shape[1]
    flat_rows = rows.reshape(slot_count, rows.shape[2])
    back_grad = lax.dot_general(
        flat_rows, weight, (((1,), (1,)), ((), ())), preferred_element_type=jnp.float32
    )
    slot_grad = jnp.sum(hidden_rows.astype(jnp.float32) * back_grad, axis=1)
    weight_col = weights.reshape(slot_count, 1).astype(jnp.float32)
    grad_hidden = (grad_scale * weight_col * back_grad).astype(jnp.bfloat16)
    weighted = (weight_col * flat_rows.astype(jnp.float32)).astype(jnp.bfloat16)
    return (slot_grad.reshape(rows.shape[0], rows.shape[1]), grad_hidden, weighted)


def weight_term(hidden_rows, weighted):
    return lax.dot_general(
        weighted, hidden_rows, (((0,), (0,)), ((), ())), preferred_element_type=jnp.float32
    )


def on_device(d_out, routes, slots, route_probs, token_counts, hidden, w_down):
    peers = lax.axis_size("expert")
    replicas = lax.axis_size("dp")
    window = peers // GROUP
    batches, tok_rows, choose = routes.shape
    slot_count = hidden.shape[2]
    capacity = slot_count // peers
    token_total = lax.psum(jnp.sum(token_counts.astype(jnp.float32)), ("dp", "expert"))
    grad_scale = batches * tok_rows * replicas * peers / token_total
    hidden_local = hidden[:, 0]
    slot_index = jnp.arange(window * capacity, dtype=jnp.int32)
    placed = jnp.where(slots >= 0, routes * capacity + slots, -1)
    matches = placed[:, None, :, :] == slot_index[None, :, None, None]
    select = (
        jnp.sum(matches, axis=3).astype(jnp.bfloat16).reshape(batches, window, capacity, tok_rows)
    )
    slot_weights = jnp.sum(
        jnp.where(matches, route_probs[:, None, :, :].astype(jnp.float32), 0.0), axis=(2, 3)
    )
    slot_weights = slot_weights.astype(jnp.bfloat16).reshape(batches, window, capacity)
    grads_hidden = []
    weighted_list = []
    returned_list = []
    for batch in range(batches):
        outgoing = jnp.einsum(
            "ect,td->ecd", select[batch], d_out[batch], preferred_element_type=jnp.float32
        ).astype(jnp.bfloat16)
        outgoing = jnp.repeat(outgoing, GROUP, axis=0)
        weights_out = jnp.repeat(slot_weights[batch], GROUP, axis=0)
        rows, weights = (
            lax.all_to_all(outgoing, "expert", split_axis=0, concat_axis=0, tiled=True),
            lax.all_to_all(weights_out, "expert", split_axis=0, concat_axis=0, tiled=True),
        )
        slot_grad, grad_hidden, weighted = expert_work(
            rows, weights, hidden_local[batch], w_down, grad_scale
        )
        returned_list.append(
            lax.all_to_all(slot_grad, "expert", split_axis=0, concat_axis=0, tiled=True)
        )
        grads_hidden.append(grad_hidden)
        weighted_list.append(weighted)
    stacked_hidden = hidden_local.reshape(batches * slot_count, hidden.shape[3])
    share = lax.psum_scatter(
        weight_term(stacked_hidden, jnp.concatenate(weighted_list, axis=0)),
        "dp",
        scatter_dimension=0,
        tiled=True,
    )
    summed_list = [
        jnp.sum(part.reshape(window, GROUP, capacity), axis=1).reshape(window * capacity)
        for part in returned_list
    ]
    d_probs = jnp.stack(
        [
            grad_scale
            * jnp.sum(jnp.where(matches[batch], summed_list[batch][:, None, None], 0.0), axis=0)
            for batch in range(batches)
        ],
        axis=0,
    )
    d_hidden = jnp.stack(grads_hidden, axis=0)[:, None]
    d_w2 = grad_scale * share
    return (d_hidden, d_w2, d_probs)


def solution(mesh):
    in_specs = (
        P(None, ("dp", "expert"), None),
        P(None, ("dp", "expert"), None),
        P(None, ("dp", "expert"), None),
        P(None, ("dp", "expert"), None),
        P(None, ("dp", "expert")),
        P(None, "dp", None, "expert"),
        P("expert", None),
    )
    out_specs = (P(None, "dp", None, "expert"), P("dp", "expert"), P(None, ("dp", "expert"), None))
    return jax.shard_map(
        on_device, mesh=mesh, in_specs=in_specs, out_specs=out_specs, check_vma=False
    )
```

profile of v0, /device:TPU:1, one launch (start us, length us, event | category | flops | bytes accessed | tf_op | source)
XLA Modules:
  0.0 367.9 jit_solution(1738023436147147492)
XLA Ops:
  7.2 0.8 convert_element_type.81
  7.9 0.7 add_select_fusion
  8.7 0.6 select_reduce_fusion
  9.2 0.1 squeeze.30
  9.3 0.6 copy.32
  10.0 17.4 %all-to-all-start.2 = ((bf16[16,1,16]{2,1,0:T(2,128)(2,1)}), bf16[16,1,16]{2,1,0:T(2,128)(2,1)S(1)}, u32[]{:S(2)}, u32[]{:S(2)}) async-start(bf16[16,1,16]{2,1,0:T(2,128)(2,1)} %copy.32), calls=%async_computation.2 | async-start | bytes 16384 | tf_op jit(solution)/shard_map/all_to_all | solution.py:59
  27.4 0.2 convert_reduce_fusion
  27.6 0.1 squeeze.27
  27.6 0.6 copy.31
  28.3 6.1 %all-to-all-done.2 = bf16[16,1,16]{2,1,0:T(2,128)(2,1)S(1)} async-done(((bf16[16,1,16]{2,1,0:T(2,128)(2,1)}), bf16[16,1,16]{2,1,0:T(2,128)(2,1)S(1)}, u32[]{:S(2)}, u32[]{:S(2)}) %all-to-all-start.2) | async-done | bytes 544 | tf_op jit(solution)/shard_map/all_to_all | solution.py:59
  34.3 3.9 %all-to-all-start = ((bf16[16,1,16]{2,1,0:T(2,128)(2,1)}), bf16[16,1,16]{2,1,0:T(2,128)(2,1)S(1)}, u32[]{:S(2)}, u32[]{:S(2)}) async-start(bf16[16,1,16]{2,1,0:T(2,128)(2,1)} %copy.31), calls=%async_computation | async-start | bytes 16384 | tf_op jit(solution)/shard_map/all_to_all | solution.py:59
  38.3 1.3 convolution_convert_fusion
  39.6 5.6 %all-to-all-done = bf16[16,1,16]{2,1,0:T(2,128)(2,1)S(1)} async-done(((bf16[16,1,16]{2,1,0:T(2,128)(2,1)}), bf16[16,1,16]{2,1,0:T(2,128)(2,1)S(1)}, u32[]{:S(2)}, u32[]{:S(2)}) %all-to-all-start) | async-done | bytes 544 | tf_op jit(solution)/shard_map/all_to_all | solution.py:59
  45.3 1.1 broadcast_in_dim.62
  46.4 4.1 %all-to-all-start.3 = ((bf16[16,16,2048]{2,1,0:T(8,128)(2,1)}), bf16[16,16,2048]{2,1,0:T(8,128)(2,1)S(1)}, u32[]{:S(2)}, u32[]{:S(2)}) async-start(bf16[16,16,2048]{2,1,0:T(8,128)(2,1)} %bitcast.11), calls=%async_computation.3 | async-start | bytes 2097152 | tf_op jit(solution)/shard_map/all_to_all | solution.py:58
  50.5 0.2 convolution_convert_fusion.1
  50.7 27.7 %all-to-all-done.3 = bf16[16,16,2048]{2,1,0:T(8,128)(2,1)S(1)} async-done(((bf16[16,16,2048]{2,1,0:T(8,128)(2,1)}), bf16[16,16,2048]{2,1,0:T(8,128)(2,1)S(1)}, u32[]{:S(2)}, u32[]{:S(2)}) %all-to-all-start.3) | async-done | bytes 1048608 | tf_op jit(solution)/shard_map/all_to_all | solution.py:58
  78.5 1.1 broadcast_in_dim.60
  79.6 3.5 all-to-all-start.1
  83.1 0.0 reduce-scatter.2.cloned.1.call-start
  83.2 0.2 copy.33
  83.5 0.1 reshape.124
  83.6 0.1 reshape.123
  83.7 1.3 multiply_convert_fusion
  85.0 26.1 %all-to-all-done.1 = bf16[16,16,2048]{2,1,0:T(8,128)(2,1)S(1)} async-done(((bf16[16,16,2048]{2,1,0:T(8,128)(2,1)}), bf16[16,16,2048]{2,1,0:T(8,128)(2,1)S(1)}, u32[]{:S(2)}, u32[]{:S(2)}) %all-to-all-start.1) | async-done | bytes 1048608 | tf_op jit(solution)/shard_map/all_to_all | solution.py:58
  111.0 0.3 multiply_convert_fusion.1
  111.3 0.9 copy-done.2
  112.2 2.1 fusion
  114.4 0.0 reduce-scatter.2.cloned.1.call-update
  114.4 0.6 copy-done.4
  115.0 0.6 convert_reduce_fusion.3
  115.6 118.0 %psum.7 = f32[]{:T(128)} all-reduce(f32[]{:T(128)} %convert_reduce_fusion.3), channel_id=1, replica_groups=mesh['dp'=64,'expert'=16] {'dp','expert'}, use_global_device_ids=true, to_apply=%region_1.0 | all-reduce | flops 1 | bytes 8 | tf_op jit(solution)/shard_map/psum | solution.py:35
  234.4 0.5 fusion.14
  234.9 0.5 fusion.9
  235.4 0.7 all_to_all.38
  236.1 5.6 %all-to-all-start.5 = ((f32[16,1,16]{2,1,0:T(1,128)}), f32[16,1,16]{2,1,0:T(1,128)S(1)}, u32[]{:S(2)}, u32[]{:S(2)}) async-start(f32[16,1,16]{2,1,0:T(1,128)} %all_to_all.38), calls=%async_computation.6 | async-start | bytes 16384 | tf_op jit(solution)/shard_map/all_to_all | solution.py:65
  241.7 0.1 iota_compare_fusion
  241.7 0.7 all_to_all.36
  242.4 6.2 %all-to-all-done.5 = f32[16,1,16]{2,1,0:T(1,128)S(1)} async-done(((f32[16,1,16]{2,1,0:T(1,128)}), f32[16,1,16]{2,1,0:T(1,128)S(1)}, u32[]{:S(2)}, u32[]{:S(2)}) %all-to-all-start.5) | async-done | bytes 1056 | tf_op jit(solution)/shard_map/all_to_all | solution.py:65
  248.6 3.9 %all-to-all-start.4 = ((f32[16,1,16]{2,1,0:T(1,128)}), f32[16,1,16]{2,1,0:T(1,128)S(1)}, u32[]{:S(2)}, u32[]{:S(2)}) async-start(f32[16,1,16]{2,1,0:T(1,128)} %all_to_all.36), calls=%async_computation.5 | async-start | bytes 16384 | tf_op jit(solution)/shard_map/all_to_all | solution.py:65
  252.5 0.7 maximum_bitcast_fusion
  253.2 0.1 broadcast_in_dim.67
  253.3 6.2 %all-to-all-done.4 = f32[16,1,16]{2,1,0:T(1,128)S(1)} async-done(((f32[16,1,16]{2,1,0:T(1,128)}), f32[16,1,16]{2,1,0:T(1,128)S(1)}, u32[]{:S(2)}, u32[]{:S(2)}) %all-to-all-start.4) | async-done | bytes 1056 | tf_op jit(solution)/shard_map/all_to_all | solution.py:65
  259.5 0.1 broadcast_in_dim.64
  259.6 0.2 select_reduce_fusion.2
  259.8 0.6 pad_maximum_fusion
  260.4 99.3 %reduce-scatter.2.cloned.1.call-done = f32[32,192]{1,0:T(8,128)} async-done(((f32[2048,192]{1,0:T(8,128)}), f32[32,192]{1,0:T(8,128)}) %reduce-scatter.2.cloned.1.call-update) | async-done | bytes 24592 | tf_op jit(solution)/shard_map/reduce_scatter | solution.py:70
  359.7 1.4 broadcast_multiply_fusion
  (21 shorter events, 0.2 us)
Async XLA Ops:
  7.2 227.2 %copy-start = (bf16[192,2048]{1,0:T(8,128)(2,1)S(1)}, bf16[192,2048]{1,0:T(8,128)(2,1)}, u32[]{:S(2)}) copy-start(bf16[192,2048]{1,0:T(8,128)(2,1)} %param.13) | copy-start | bytes 2359300
  10.0 24.4 %all-to-all-start.2 = ((bf16[16,1,16]{2,1,0:T(2,128)(2,1)}), bf16[16,1,16]{2,1,0:T(2,128)(2,1)S(1)}, u32[]{:S(2)}, u32[]{:S(2)}) async-start(bf16[16,1,16]{2,1,0:T(2,128)(2,1)} %copy.32), calls=%async_computation.2 | async-start | bytes 16384 | tf_op jit(solution)/shard_map/all_to_all | solution.py:59
  34.3 10.9 %all-to-all-start = ((bf16[16,1,16]{2,1,0:T(2,128)(2,1)}), bf16[16,1,16]{2,1,0:T(2,128)(2,1)S(1)}, u32[]{:S(2)}, u32[]{:S(2)}) async-start(bf16[16,1,16]{2,1,0:T(2,128)(2,1)} %copy.31), calls=%async_computation | async-start | bytes 16384 | tf_op jit(solution)/shard_map/all_to_all | solution.py:59
  38.3 12.2 %copy-start.1 = (bf16[2,128,2048]{2,1,0:T(8,128)(2,1)S(1)}, bf16[2,128,2048]{2,1,0:T(8,128)(2,1)}, u32[]{:S(2)}) copy-start(bf16[2,128,2048]{2,1,0:T(8,128)(2,1)} %param.7) | copy-start | bytes 3145732
  46.4 32.1 %all-to-all-start.3 = ((bf16[16,16,2048]{2,1,0:T(8,128)(2,1)}), bf16[16,16,2048]{2,1,0:T(8,128)(2,1)S(1)}, u32[]{:S(2)}, u32[]{:S(2)}) async-start(bf16[16,16,2048]{2,1,0:T(8,128)(2,1)} %bitcast.11), calls=%async_computation.3 | async-start | bytes 2097152 | tf_op jit(solution)/shard_map/all_to_all | solution.py:58
  50.5 32.7 %copy-start.3 = (bf16[2,1,256,192]{2,3,1,0:T(8,128)(2,1)S(1)}, bf16[2,1,256,192]{2,3,1,0:T(8,128)(2,1)}, u32[]{:S(2)}) copy-start(bf16[2,1,256,192]{2,3,1,0:T(8,128)(2,1)} %param.12) | copy-start | bytes 589828
  79.6 31.5 %all-to-all-start.1 = ((bf16[16,16,2048]{2,1,0:T(8,128)(2,1)}), bf16[16,16,2048]{2,1,0:T(8,128)(2,1)S(1)}, u32[]{:S(2)}, u32[]{:S(2)}) async-start(bf16[16,16,2048]{2,1,0:T(8,128)(2,1)} %bitcast.60), calls=%async_computation.1 | async-start | bytes 2097152 | tf_op jit(solution)/shard_map/all_to_all | solution.py:58
  83.1 276.6 %reduce-scatter.2.cloned.1.call-start = ((), (), s32[]{:S(2)}) async-start(), calls=%async_computation.7 | async-start | bytes 2129920 | tf_op jit(solution)/shard_map/reduce_scatter | solution.py:70
  111.0 1.2 copy-start.2
  114.4 0.7 copy-start.4
  236.1 12.5 %all-to-all-start.5 = ((f32[16,1,16]{2,1,0:T(1,128)}), f32[16,1,16]{2,1,0:T(1,128)S(1)}, u32[]{:S(2)}, u32[]{:S(2)}) async-start(f32[16,1,16]{2,1,0:T(1,128)} %all_to_all.38), calls=%async_computation.6 | async-start | bytes 16384 | tf_op jit(solution)/shard_map/all_to_all | solution.py:65
  248.6 10.9 %all-to-all-start.4 = ((f32[16,1,16]{2,1,0:T(1,128)}), f32[16,1,16]{2,1,0:T(1,128)S(1)}, u32[]{:S(2)}, u32[]{:S(2)}) async-start(f32[16,1,16]{2,1,0:T(1,128)} %all_to_all.36), calls=%async_computation.5 | async-start | bytes 16384 | tf_op jit(solution)/shard_map/all_to_all | solution.py:65
Sparse Core Ops, SparseCore 0:
  114.5 245.1 reduce-scatter.1
where the time goes:
time: 372 us; the launch traced here: 368 us
  waiting for transfers between devices  177 us (48%)
  blocking collectives  118 us (32%)
  starting transfers between devices  38.5 us (10%)
  between operations  14.9 us (4%)
  other arithmetic  7.44 us (2%)
  local copies, waits for them, and re-layouts  7.19 us (2%)
  matrix products  4.7 us (1%)
    psum x1, blocking collectives, on_device(): lax.psum(jnp.sum(token_counts.astype(jnp.float32)), ('dp', 'expert'))  118 us
    reduce_scatter x1, waiting for transfers between devices, on_device(): lax.psum_scatter(weight_term(stacked_hidden, jnp.concatenate(weighted_lis...  99.3 us
    all_to_all x2, waiting for transfers between devices, on_device(): lax.all_to_all(outgoing, 'expert', split_axis=0, concat_axis=0, tiled=True)  53.8 us
    all_to_all x2, starting transfers between devices, on_device(): lax.all_to_all(weights_out, 'expert', split_axis=0, concat_axis=0, tiled=...  21.3 us
    all_to_all x2, waiting for transfers between devices, on_device(): lax.all_to_all(slot_grad, 'expert', split_axis=0, concat_axis=0, tiled=True)  12.4 us
    all_to_all x2, waiting for transfers between devices, on_device(): lax.all_to_all(weights_out, 'expert', split_axis=0, concat_axis=0, tiled=...  11.7 us
    all_to_all x2, starting transfers between devices, on_device(): lax.all_to_all(slot_grad, 'expert', split_axis=0, concat_axis=0, tiled=True)  9.47 us
    all_to_all x2, starting transfers between devices, on_device(): lax.all_to_all(outgoing, 'expert', split_axis=0, concat_axis=0, tiled=True)  7.66 us
  transfers between devices with their start and end apart: 7, of which 7 were waited for; matrix products, arithmetic and copies ran while one was open for 2% of the time, Pallas kernels for 0%

commit v1 on v0

v1 whole, which is shorter than its diff:
```python
import functools
import math

import jax
import jax.numpy as jnp
from jax import lax
from jax.experimental import pallas as pl
from jax.experimental.pallas import tpu as pltpu
from jax.sharding import PartitionSpec as P

MESH = pl.DeviceIdType.MESH
F32 = jnp.float32
BF16 = jnp.bfloat16
RING = 8
GROUP = 4
AHEAD = 2


def iota(shape, dimension):
    return lax.broadcasted_iota(jnp.int32, shape, dimension)


def kernel(
    nz, nx, scale_top,
    dout_ref, routes_ref, slots_ref, probs_ref, counts_ref, hid_ref, w_ref,
    dh_ref, dw_ref, dp_ref,
    sel, out, outw, rows, roww, wmat, wrow, back, ht, xs, xr, zs, zr, cs, cxr, czr, rs, rr,
    near_s, near_r, mate_s, mate_r, sib_s, sib_r, x_s, x_r, z_s, z_r, c_s, c_r, ret_s, ret_r,
):
    d = lax.axis_index("dp")
    j = lax.axis_index("expert")
    z, x = lax.div(d, nx), lax.rem(d, nx)
    y, c = lax.div(j, 2), lax.rem(j, 2)
    sign = 2 * lax.rem(y, 2) - 1
    mine = lax.div(y, 2)
    batches, choose, toks = routes_ref.shape
    hidden = w_ref.shape[0]
    cap = out.shape[3]
    cw = out.shape[4]
    peers = 2 * RING
    window = peers // GROUP
    slot_rows = window * cap
    total_rows = batches * peers * cap

    def along_y(offset):
        return lax.rem(y + offset + 2 * RING, RING)

    mate_y = y - sign
    mate = (d, mate_y * 2 + c)
    sibling = (d, y * 2 + 1 - c)
    sources = [along_y(sign * k) for k in (1, 2, 3)]
    targets = [along_y(sign * k) for k in (1, -2, 3)]

    barrier = pltpu.get_barrier_semaphore()

    def greet(target):
        pl.semaphore_signal(barrier, inc=1, device_id=target, device_id_type=MESH)

    for k in range(1, peers):
        greet((d, lax.rem(j + k, peers)))
    for k in range(1, nx):
        greet((z * nx + lax.rem(x + k, nx), j))
    for k in range(1, nz):
        greet((lax.rem(z + k, nz) * nx + x, j))

    def placed(batch):
        chosen = slots_ref[batch]
        return jnp.where(chosen >= 0, routes_ref[batch] * cap + chosen, -1)

    for batch in range(batches):
        place = placed(batch)
        probs = probs_ref[batch].astype(F32)
        at = iota((slot_rows, toks), 0)
        picked = jnp.zeros((slot_rows, toks), F32)
        weight = jnp.zeros((slot_rows, toks), F32)
        for k in range(choose):
            same = at == place[k : k + 1, :]
            picked = jnp.where(same, 1.0, picked)
            weight = jnp.where(same, probs[k : k + 1, :], weight)
        sel[batch] = picked.astype(BF16)
        column = jnp.sum(weight, axis=1, keepdims=True)
        count = counts_ref[0, batch].astype(F32)
        block = jnp.where(iota((slot_rows, 128), 1) < 64, column, count)
        outw[:, batch] = block.astype(BF16).reshape(window, cap, 128)
    roww[:, y, c] = outw[mine]

    def remote(src, dst, send, recv, target):
        return pltpu.make_async_remote_copy(
            src_ref=src, dst_ref=dst, send_sem=send, recv_sem=recv, device_id=target, device_id_type=MESH
        )

    def send_own(source, target, step):
        for k in range(3):
            remote(
                source.at[lax.div(targets[k], 2)], target.at[:, y, c],
                near_s.at[step, k], near_r.at[step, k], (d, targets[k] * 2 + c),
            ).start()
        remote(source.at[mine], target.at[:, y, c], mate_s.at[step, 0], mate_r.at[step, 0], mate).start()

    def pass_near(target, step):
        for k in range(3):
            held = target.at[:, sources[k], c]
            remote(held, held, near_s.at[step, k], near_r.at[step, k], mate).wait_recv()
            remote(held, held, mate_s.at[step, k + 1], mate_r.at[step, k + 1], mate).start()

    def pass_mate(target, step):
        for k in range(4):
            held = target.at[:, along_y(-sign * (k + 1)), c]
            remote(held, held, mate_s.at[step, k], mate_r.at[step, k], mate).wait_recv()
        half = target.at[:, :, c]
        remote(half, half, sib_s.at[step], sib_r.at[step], sibling).start()

    def take_sibling(target, step):
        half = target.at[:, :, 1 - c]
        remote(half, half, sib_s.at[step], sib_r.at[step], sibling).wait_recv()

    def finish_sends(source, target, step):
        for k in range(3):
            remote(source.at[0], source.at[0], near_s.at[step, k], near_r.at[step, k], mate).wait_send()
        for k in range(4):
            remote(source.at[0], source.at[0], mate_s.at[step, k], mate_r.at[step, k], mate).wait_send()
        half = target.at[:, :, c]
        remote(half, half, sib_s.at[step], sib_r.at[step], sibling).wait_send()

    def owner(step):
        return lax.rem(z + 1 + step, nz)

    def columns(step):
        return pl.ds(pl.multiple_of(owner(step) * cw, cw), cw)

    def prepare(step):
        for batch in range(batches):
            block = jnp.dot(sel[batch], dout_ref[batch, :, columns(step)], preferred_element_type=F32)
            out[step, :, batch] = block.astype(BF16).reshape(window, cap, cw)
        rows[step, :, y, c] = out[step, mine]

    def compute(step):
        held = rows[step].reshape(total_rows, cw)
        back[...] += lax.dot_general(
            w_ref[:, columns(step)], held, (((1,), (1,)), ((), ())), preferred_element_type=F32
        )
        wide = jnp.concatenate([wmat[...]] * (cw // 128), axis=1) if cw > 128 else wmat[:, :cw]
        weighted = (wide * held.astype(F32)).astype(BF16)
        term = jnp.dot(ht[...], weighted, preferred_element_type=F32)
        flat = jnp.transpose(term)
        depth = cw // nx
        first = flat[:, :128].reshape(nx, depth, 128)
        last = flat[:, 128:].reshape(nx, 2, depth // 2, hidden - 128)
        packed = jnp.concatenate([last[:, 0], last[:, 1]], axis=-1)
        xs[step] = jnp.concatenate([first, packed], axis=1).astype(BF16)
        for k in range(1, nx):
            there = lax.rem(x + k, nx)
            remote(
                xs.at[step, there], xr.at[step, k - 1], x_s.at[step], x_r.at[step], (z * nx + there, j)
            ).start()

    def combine(step):
        remote(xr.at[step], xr.at[step], x_s.at[step], x_r.at[step], mate).wait_recv()
        summed = xs[step, x].astype(F32)
        for k in range(nx - 1):
            summed = summed + xr[step, k].astype(F32)
        zs[step] = summed

    def send_z(step):
        remote(zs.at[step], zr.at[step], z_s.at[step], z_r.at[step], (owner(step) * nx + x, j)).start()

    for step in range(AHEAD):
        prepare(step)
    for batch in range(batches):
        width = peers * cap
        ht[:, batch * width : (batch + 1) * width] = hid_ref[batch]
    back[...] = jnp.zeros_like(back)

    pl.semaphore_wait(barrier, peers - 1 + nx - 1 + nz - 1)
    send_own(outw, roww, nz)
    for step in range(AHEAD):
        send_own(out.at[step], rows.at[step], step)
    pass_near(roww, nz)
    pass_mate(roww, nz)

    def weights_arrive():
        take_sibling(roww, nz)
        flat = roww[...].reshape(total_rows, 128)
        wide = flat.astype(F32)
        wmat[...] = jnp.broadcast_to(wide[:, 0:1], wmat.shape)
        first = (iota((8, 128), 1) == 0).astype(BF16)
        wrow[...] = lax.dot_general(first, flat, (((1,), (1,)), ((), ())), preferred_element_type=F32)
        count = jnp.sum(wide[:, 64:65], axis=0, keepdims=True) * (1.0 / cap)
        cs[0] = jnp.broadcast_to(count, cs.shape[1:])
        for k in range(1, nx):
            remote(cs.at[0], cxr.at[k - 1], c_s.at[0], c_r.at[0], (z * nx + lax.rem(x + k, nx), j)).start()

    def counts_second():
        remote(cxr, cxr, c_s.at[0], c_r.at[0], mate).wait_recv()
        cs[1] = cs[0] + jnp.sum(cxr[...], axis=0)
        for k in range(1, nz):
            remote(cs.at[1], czr.at[k - 1], c_s.at[1], c_r.at[1], (lax.rem(z + k, nz) * nx + x, j)).start()

    def body(i, carry):
        @pl.when(i + AHEAD < nz)
        def _():
            prepare(i + AHEAD)
            send_own(out.at[i + AHEAD], rows.at[i + AHEAD], i + AHEAD)

        @pl.when(i < nz)
        def _():
            pass_near(rows.at[i], i)

        @pl.when((i >= 1) & (i < nz + 1))
        def _():
            pass_mate(rows.at[i - 1], i - 1)

        @pl.when(i == 1)
        def _():
            weights_arrive()

        @pl.when(i == min(4, nz))
        def _():
            counts_second()

        @pl.when((i >= 2) & (i < nz + 2))
        def _():
            take_sibling(rows.at[i - 2], i - 2)
            compute(i - 2)

        @pl.when((i >= 3) & (i < nz + 2))
        def _():
            combine(i - 3)
            send_z(i - 3)

        return carry

    lax.fori_loop(0, nz + 2, body, 0)

    grads = back[...]
    partial = jnp.sum(ht[...].astype(F32) * grads, axis=0, keepdims=True)
    lane = iota((peers, total_rows), 1)
    spread = jnp.where(lax.rem(lax.div(lane, cap), peers) == iota((peers, total_rows), 0), partial, 0.0)
    row = iota((total_rows, 128), 0)
    place = mine * (batches * cap) + lax.div(row, peers * cap) * cap + lax.rem(row, cap)
    gather = (iota((total_rows, 128), 1) == place).astype(F32)
    back_rows = jnp.dot(spread, gather, precision=lax.Precision.HIGHEST, preferred_element_type=F32)
    for k in range(peers):
        rs[k] = back_rows[k : k + 1, :]
    for k in range(1, peers):
        there = lax.rem(j + k, peers)
        remote(rs.at[there], rr.at[k - 1], ret_s, ret_r, (d, there)).start()

    remote(czr, czr, c_s.at[1], c_r.at[1], mate).wait_recv()
    token_total = jnp.sum((cs[1] + jnp.sum(czr[...], axis=0))[0:1, 0:1], axis=0, keepdims=True)
    grad_scale = scale_top / token_total

    scaled = ((grad_scale * wrow[0:1, :]) * grads).astype(BF16)
    for batch in range(batches):
        width = peers * cap
        dh_ref[batch] = scaled[:, batch * width : (batch + 1) * width]

    combine(nz - 1)
    for step in range(nz - 1):
        remote(zr.at[step], zr.at[step], z_s.at[step], z_r.at[step], mate).wait_recv()
    share = zs[nz - 1]
    for step in range(nz - 1):
        share = share + zr[step]
    share = grad_scale * share
    depth = dw_ref.shape[0]
    dw_ref[:, :128] = share[:depth]
    dw_ref[: depth // 2, 128:] = share[depth:, : hidden - 128]
    dw_ref[depth // 2 :, 128:] = share[depth:, hidden - 128 :]

    remote(rr, rr, ret_s, ret_r, mate).wait_recv()
    totals = rs[j]
    for k in range(peers - 1):
        totals = totals + rr[k]
    diagonal = iota((128, 128), 0) == iota((128, 128), 1)
    column = jnp.sum(jnp.where(diagonal, totals, 0.0), axis=1, keepdims=True)
    for batch in range(batches):
        place = placed(batch)
        mine_column = jnp.concatenate(
            [column[(e * batches + batch) * cap : (e * batches + batch + 1) * cap] for e in range(window)], axis=0
        )
        at = iota((slot_rows, toks), 0)
        for k in range(choose):
            found = jnp.sum(jnp.where(at == place[k : k + 1, :], mine_column, 0.0), axis=0, keepdims=True)
            dp_ref[batch, k : k + 1, :] = grad_scale * found

    finish_sends(outw, roww, nz)
    for step in range(nz):
        finish_sends(out.at[step], rows.at[step], step)
        remote(xr.at[step], xr.at[step], x_s.at[step], x_r.at[step], mate).wait_send()
    for step in range(nz - 1):
        remote(zs.at[step], zs.at[step], z_s.at[step], z_r.at[step], mate).wait_send()
    remote(cxr, cxr, c_s.at[0], c_r.at[0], mate).wait_send()
    remote(czr, czr, c_s.at[1], c_r.at[1], mate).wait_send()
    remote(rr, rr, ret_s, ret_r, mate).wait_send()


def on_device(nz, nx, d_out, routes, slots, route_probs, token_counts, hidden, w_down):
    batches, toks, choose = routes.shape
    features = d_out.shape[2]
    units, slot_count = hidden.shape[3], hidden.shape[2]
    peers = 2 * RING
    cap = slot_count // peers
    window = peers // GROUP
    cw = features // nz
    total_rows = batches * slot_count
    piece = (features // (nz * nx)) * units // 128
    scale_top = float(batches * toks * nz * nx * peers)
    dma = pltpu.SemaphoreType.DMA
    vmem = pl.BlockSpec(memory_space=pltpu.VMEM)
    dh, dw, dp = pl.pallas_call(
        functools.partial(kernel, nz, nx, scale_top),
        out_shape=(
            jax.ShapeDtypeStruct((batches, units, slot_count), BF16),
            jax.ShapeDtypeStruct((features // (nz * nx), units), F32),
            jax.ShapeDtypeStruct((batches, choose, toks), F32),
        ),
        in_specs=[vmem] * 4 + [pl.BlockSpec(memory_space=pltpu.SMEM)] + [vmem] * 2,
        out_specs=[vmem] * 3,
        scratch_shapes=[
            pltpu.VMEM((batches, window * cap, toks), BF16),
            pltpu.VMEM((nz, window, batches, cap, cw), BF16),
            pltpu.VMEM((window, batches, cap, 128), BF16),
            pltpu.VMEM((nz, batches, RING, 2, cap, cw), BF16),
            pltpu.VMEM((batches, RING, 2, cap, 128), BF16),
            pltpu.VMEM((total_rows, 128), F32),
            pltpu.VMEM((8, total_rows), F32),
            pltpu.VMEM((units, total_rows), F32),
            pltpu.VMEM((units, total_rows), BF16),
            pltpu.VMEM((nz, nx, piece, 128), BF16),
            pltpu.VMEM((nz, nx - 1, piece, 128), BF16),
            pltpu.VMEM((nz, piece, 128), F32),
            pltpu.VMEM((nz - 1, piece, 128), F32),
            pltpu.VMEM((2, 8, 128), F32),
            pltpu.VMEM((nx - 1, 8, 128), F32),
            pltpu.VMEM((nz - 1, 8, 128), F32),
            pltpu.VMEM((peers, 1, 128), F32),
            pltpu.VMEM((peers - 1, 1, 128), F32),
            dma((nz + 1, 3)), dma((nz + 1, 3)), dma((nz + 1, 4)), dma((nz + 1, 4)),
            dma((nz + 1,)), dma((nz + 1,)), dma((nz,)), dma((nz,)),
            dma((nz,)), dma((nz,)), dma((2,)), dma((2,)), dma, dma,
        ],
        compiler_params=pltpu.CompilerParams(
            collective_id=0, has_side_effects=True, vmem_limit_bytes=32 * 1024 * 1024
        ),
    )(
        d_out,
        jnp.swapaxes(routes, 1, 2),
        jnp.swapaxes(slots, 1, 2),
        jnp.swapaxes(route_probs, 1, 2),
        jnp.swapaxes(token_counts, 0, 1),
        jnp.swapaxes(hidden[:, 0], 1, 2),
        w_down,
    )
    return jnp.swapaxes(dh, 1, 2)[:, None], dw, jnp.swapaxes(dp, 1, 2)


def solution(mesh):
    nx = math.isqrt(mesh.shape["dp"])
    nz = mesh.shape["dp"] // nx
    both = ("dp", "expert")
    in_specs = (
        P(None, both, None),
        P(None, both, None),
        P(None, both, None),
        P(None, both, None),
        P(None, both),
        P(None, "dp", None, "expert"),
        P("expert", None),
    )
    out_specs = (P(None, "dp", None, "expert"), P("dp", "expert"), P(None, both, None))
    return jax.shard_map(
        functools.partial(on_device, nz, nx), mesh=mesh, in_specs=in_specs, out_specs=out_specs, check_vma=False
    )
```

time: 372 us -> 77.6 us (0.21)
  waiting for transfers between devices: 177 us -> 0 us
  blocking collectives: 118 us -> 0 us
  Pallas kernels: 0 us -> 69.3 us
  starting transfers between devices: 38.5 us -> 0 us
  between operations: 14.9 us -> 0.66 us
  other arithmetic: 7.44 us -> 0 us
  matrix products: 4.7 us -> 0 us
    psum x1 -> x0, blocking collectives: 118 us -> none  [on_device(): lax.psum(jnp.sum(token_counts.astype(jnp.float32)), ('dp', 'expert'))]
    reduce_scatter x1 -> x0, waiting for transfers between devices: 99.3 us -> none  [on_device(): lax.psum_scatter(weight_term(stacked_hidden, jnp.concatenate(weighted_lis...]
    all_to_all x6 -> x0, waiting for transfers between devices: 77.9 us -> none  [the longest x2 53.8 us: on_device(): lax.all_to_all(outgoing, 'expert', split_axis=0, concat_axis=0, tiled=True)]
    pallas_call x0 -> x1, Pallas kernels: none -> 69.3 us  [on_device(): pl.pallas_call(functools.partial(kernel, nz, nx, scale_top), out_shape=(j...]
    all_to_all x6 -> x0, starting transfers between devices: 38.5 us -> none  [the longest x2 21.3 us: on_device(): lax.all_to_all(weights_out, 'expert', split_axis=0, concat_axis=0, tiled=...]
    unnamed x12 -> x17, local copies, waits for them, and re-layouts: 1.83 us -> 7.24 us
    dot_general x5 -> x0, matrix products: 4.7 us -> none  [the longest x1 2.11 us: weight_term(): lax.dot_general(weighted, hidden_rows, (((0,), (0,)), ((), ())), preferre...]
  transfers between devices with their start and end apart: 7 -> 0, of which waited for: 7 -> 0; matrix products, arithmetic and copies ran while one was open for 2% -> 0% of each run, Pallas kernels for 0% -> 0%
where the time goes in v1:
time: 77.6 us; the launch traced here: 77.2 us
  Pallas kernels  69.3 us (89%)
  local copies, waits for them, and re-layouts  7.24 us (9%)
    pallas_call x1, Pallas kernels, on_device(): pl.pallas_call(functools.partial(kernel, nz, nx, scale_top), out_shape=(j...  69.3 us
    unnamed x17, local copies, waits for them, and re-layouts  7.24 us

profile of v1, /device:TPU:1, one launch (start us, length us, event | category | flops | bytes accessed | tf_op | source)
XLA Modules:
  0.0 77.2 jit_solution(7969723347150657089)
XLA Ops:
  0.6 0.0 copy-start.3
  0.6 0.0 copy-start.6
  0.7 0.7 copy-done.3
  1.3 0.0 copy-done.6
  1.3 0.0 copy-start
  1.3 1.2 %copy-done = bf16[2,128,2048]{2,1,0:T(8,128)(2,1)S(1)} copy-done((bf16[2,128,2048]{2,1,0:T(8,128)(2,1)S(1)}, bf16[2,128,2048]{2,1,0:T(8,128)(2,1)}, u32[]{:S(2)}) %copy-start) | copy-done | bytes 1048600
  2.6 0.0 copy-start.1
  2.6 1.1 %copy-done.1 = bf16[192,2048]{1,0:T(8,128)(2,1)S(1)} copy-done((bf16[192,2048]{1,0:T(8,128)(2,1)S(1)}, bf16[192,2048]{1,0:T(8,128)(2,1)}, u32[]{:S(2)}) %copy-start.1) | copy-done | bytes 786456
  3.7 0.0 copy-start.2
  3.7 0.9 %copy-done.2 = bf16[2,1,256,192]{2,3,1,0:T(8,128)(2,1)S(1)} copy-done((bf16[2,1,256,192]{2,3,1,0:T(8,128)(2,1)S(1)}, bf16[2,1,256,192]{2,3,1,0:T(8,128)(2,1)}, u32[]{:S(2)}) %copy-start.2) | copy-done | bytes 196632
  4.6 0.0 copy-start.4
  4.6 0.7 copy-done.4
  5.3 0.0 copy-start.5
  5.3 0.7 copy-done.5
  6.0 69.3 %shard_map.94 = (bf16[2,192,256]{2,1,0:T(8,128)(2,1)S(1)}, f32[32,192]{1,0:T(8,128)S(1)}, f32[2,8,128]{2,1,0:T(8,128)S(1)}) custom-call(bf16[2,128,2048]{2,1,0:T(8,128)(2,1)S(1)} %copy-done, s32[2,8,128]{2,1,0:T(8,128)S(1)} %bitcast.15, s32[2,8,128]{2,1,0:T(8,128)S(1)} %bitcast.16, bf16[2,8,128]{2,1,0:T(8,128)(2,1)S(1)} %bitcast.18, s32[1,2]{1,0:T(1,128)S(1)} %bitcast.19, ...), custom_call_target="tpu_custom_call" | custom-call | tf_op jit(solution)/shard_map/pallas_call | solution.py:310
  75.3 0.7 copy.14
  76.0 0.6 copy.15
  76.6 0.6 copy.16
Async XLA Ops:
  0.6 0.7 copy-start.3
  0.6 0.7 copy-start.6
  1.3 1.2 %copy-start = (bf16[2,128,2048]{2,1,0:T(8,128)(2,1)S(1)}, bf16[2,128,2048]{2,1,0:T(8,128)(2,1)}, u32[]{:S(2)}) copy-start(bf16[2,128,2048]{2,1,0:T(8,128)(2,1)} %dout_ref.1) | copy-start | bytes 3145732
  2.6 1.1 %copy-start.1 = (bf16[192,2048]{1,0:T(8,128)(2,1)S(1)}, bf16[192,2048]{1,0:T(8,128)(2,1)}, u32[]{:S(2)}) copy-start(bf16[192,2048]{1,0:T(8,128)(2,1)} %w_ref.1) | copy-start | bytes 2359300
  3.7 0.9 %copy-start.2 = (bf16[2,1,256,192]{2,3,1,0:T(8,128)(2,1)S(1)}, bf16[2,1,256,192]{2,3,1,0:T(8,128)(2,1)}, u32[]{:S(2)}) copy-start(bf16[2,1,256,192]{2,3,1,0:T(8,128)(2,1)} %param.12) | copy-start | bytes 589828
  4.6 0.7 copy-start.4
  5.3 0.7 copy-start.5

commit v2 on v1

--- a/solution.py
+++ b/solution.py
@@ -13,7 +13,10 @@
 BF16 = jnp.bfloat16
 RING = 8
 GROUP = 4
-AHEAD = 2
+AHEAD = 8
+MATE_LAG = 2
+SIB_LAG = 1
+SUM_LAG = 6
 
 
 def iota(shape, dimension):
@@ -22,10 +25,11 @@
 
 def kernel(
     nz, nx, scale_top,
-    dout_ref, routes_ref, slots_ref, probs_ref, counts_ref, hid_ref, w_ref,
+    dout_hbm, routes_hbm, slots_hbm, probs_hbm, counts_ref, hid_hbm, w_hbm,
     dh_ref, dw_ref, dp_ref,
-    sel, out, outw, rows, roww, wmat, wrow, back, ht, xs, xr, zs, zr, cs, cxr, czr, rs, rr,
-    near_s, near_r, mate_s, mate_r, sib_s, sib_r, x_s, x_r, z_s, z_r, c_s, c_r, ret_s, ret_r,
+    dout_ref, routes_ref, slots_ref, probs_ref, ht, w_ref, in_sem,
+    sel, out, outw, rows, roww, wmat, wrow, back, spot, xs, xr, zs, zr, zb, zbr, zx, zxr, cs, cxr, czr, rs, rr,
+    near_s, near_r, mate_s, mate_r, sib_s, sib_r, x_s, x_r, z_s, z_r, b_s, b_r, f_s, f_r, c_s, c_r, ret_s, ret_r,
 ):
     d = lax.axis_index("dp")
     j = lax.axis_index("expert")
@@ -51,6 +55,18 @@
     sources = [along_y(sign * k) for k in (1, 2, 3)]
     targets = [along_y(sign * k) for k in (1, -2, 3)]
 
+    width = peers * cap
+    loads = [
+        pltpu.make_async_copy(src, dst, in_sem.at[k])
+        for k, (src, dst) in enumerate(
+            [(routes_hbm, routes_ref), (slots_hbm, slots_ref), (probs_hbm, probs_ref), (dout_hbm, dout_ref)]
+            + [(hid_hbm.at[batch], ht.at[:, batch * width : (batch + 1) * width]) for batch in range(batches)]
+            + [(w_hbm, w_ref)]
+        )
+    ]
+    for load in loads:
+        load.start()
+
     barrier = pltpu.get_barrier_semaphore()
 
     def greet(target):
@@ -67,6 +83,9 @@
         chosen = slots_ref[batch]
         return jnp.where(chosen >= 0, routes_ref[batch] * cap + chosen, -1)
 
+    for load in loads[:3]:
+        load.wait()
+    weights = []
     for batch in range(batches):
         place = placed(batch)
         probs = probs_ref[batch].astype(F32)
@@ -78,11 +97,16 @@
             picked = jnp.where(same, 1.0, picked)
             weight = jnp.where(same, probs[k : k + 1, :], weight)
         sel[batch] = picked.astype(BF16)
-        column = jnp.sum(weight, axis=1, keepdims=True)
-        count = counts_ref[0, batch].astype(F32)
-        block = jnp.where(iota((slot_rows, 128), 1) < 64, column, count)
-        outw[:, batch] = block.astype(BF16).reshape(window, cap, 128)
-    roww[:, y, c] = outw[mine]
+        weights.append(weight)
+
+    def send_weights():
+        for batch in range(batches):
+            column = jnp.sum(weights[batch], axis=1, keepdims=True)
+            count = counts_ref[0, batch].astype(F32)
+            block = jnp.where(iota((slot_rows, 128), 1) < 64, column, count)
+            outw[:, batch] = block.astype(BF16).reshape(window, cap, 128)
+        roww[:, y, c] = outw[mine]
+        send_own(outw, roww, nz)
 
     def remote(src, dst, send, recv, target):
         return pltpu.make_async_remote_copy(
@@ -147,12 +171,17 @@
         first = flat[:, :128].reshape(nx, depth, 128)
         last = flat[:, 128:].reshape(nx, 2, depth // 2, hidden - 128)
         packed = jnp.concatenate([last[:, 0], last[:, 1]], axis=-1)
-        xs[step] = jnp.concatenate([first, packed], axis=1).astype(BF16)
+        xs[step] = first.astype(BF16)
+        zb[step] = packed.astype(BF16)
         for k in range(1, nx):
             there = lax.rem(x + k, nx)
             remote(
                 xs.at[step, there], xr.at[step, k - 1], x_s.at[step], x_r.at[step], (z * nx + there, j)
             ).start()
+
+        @pl.when(step < nz - 1)
+        def _():
+            remote(zb.at[step], zbr.at[step], b_s.at[step], b_r.at[step], (owner(step) * nx + x, j)).start()
 
     def combine(step):
         remote(xr.at[step], xr.at[step], x_s.at[step], x_r.at[step], mate).wait_recv()
@@ -164,19 +193,21 @@
     def send_z(step):
         remote(zs.at[step], zr.at[step], z_s.at[step], z_r.at[step], (owner(step) * nx + x, j)).start()
 
-    for step in range(AHEAD):
+    loads[3].wait()
+    prepare(0)
+    pl.semaphore_wait(barrier, peers - 1 + nx - 1 + nz - 1)
+    send_own(out.at[0], rows.at[0], 0)
+    send_weights()
+    for step in range(1, min(AHEAD, nz)):
         prepare(step)
-    for batch in range(batches):
-        width = peers * cap
-        ht[:, batch * width : (batch + 1) * width] = hid_ref[batch]
+        send_own(out.at[step], rows.at[step], step)
     back[...] = jnp.zeros_like(back)
-
-    pl.semaphore_wait(barrier, peers - 1 + nx - 1 + nz - 1)
-    send_own(outw, roww, nz)
-    for step in range(AHEAD):
-        send_own(out.at[step], rows.at[step], step)
-    pass_near(roww, nz)
-    pass_mate(roww, nz)
+    row = iota((total_rows, 128), 0)
+    shift, mask = cap.bit_length() - 1, cap - 1
+    place = mine * (batches * cap) + (row >> (2 * shift)) * cap + (row & mask)
+    spot[...] = (iota((total_rows, 128), 1) == place).astype(F32)
+    for load in loads[4:]:
+        load.wait()
 
     def weights_arrive():
         take_sibling(roww, nz)
@@ -197,49 +228,72 @@
             remote(cs.at[1], czr.at[k - 1], c_s.at[1], c_r.at[1], (lax.rem(z + k, nz) * nx + x, j)).start()
 
     def body(i, carry):
-        @pl.when(i + AHEAD < nz)
-        def _():
-            prepare(i + AHEAD)
-            send_own(out.at[i + AHEAD], rows.at[i + AHEAD], i + AHEAD)
+        if AHEAD < nz:
+
+            @pl.when(i + AHEAD < nz)
+            def _():
+                prepare(i + AHEAD)
+                send_own(out.at[i + AHEAD], rows.at[i + AHEAD], i + AHEAD)
 
         @pl.when(i < nz)
         def _():
             pass_near(rows.at[i], i)
 
-        @pl.when((i >= 1) & (i < nz + 1))
-        def _():
-            pass_mate(rows.at[i - 1], i - 1)
-
-        @pl.when(i == 1)
+        @pl.when(i == 0)
+        def _():
+            pass_near(roww, nz)
+
+        held = i - MATE_LAG
+
+        @pl.when((held >= 0) & (held < nz))
+        def _():
+            pass_mate(rows.at[held], held)
+
+        @pl.when(held == 0)
+        def _():
+            pass_mate(roww, nz)
+
+        whole = held - SIB_LAG
+
+        @pl.when(whole == 0)
         def _():
             weights_arrive()
 
-        @pl.when(i == min(4, nz))
+        @pl.when(i == nz)
         def _():
             counts_second()
 
-        @pl.when((i >= 2) & (i < nz + 2))
-        def _():
-            take_sibling(rows.at[i - 2], i - 2)
-            compute(i - 2)
-
-        @pl.when((i >= 3) & (i < nz + 2))
-        def _():
-            combine(i - 3)
-            send_z(i - 3)
+        @pl.when((whole >= 0) & (whole < nz))
+        def _():
+            take_sibling(rows.at[whole], whole)
+            compute(whole)
+
+        done = whole - SUM_LAG
+
+        @pl.when((done >= 0) & (done < nz - 1))
+        def _():
+            combine(done)
+            send_z(done)
 
         return carry
 
-    lax.fori_loop(0, nz + 2, body, 0)
+    lax.fori_loop(0, nz + max(MATE_LAG + SIB_LAG, MATE_LAG + SIB_LAG + SUM_LAG - 1), body, 0)
+
+    for step in range(nz - 1):
+        remote(zbr.at[step], zbr.at[step], b_s.at[step], b_r.at[step], mate).wait_recv()
+    block = zb[nz - 1].astype(F32)
+    for step in range(nz - 1):
+        block = block + zbr[step].astype(F32)
+    zx[...] = block
+    for k in range(1, nx):
+        there = lax.rem(x + k, nx)
+        remote(zx.at[there], zxr.at[k - 1], f_s, f_r, (z * nx + there, j)).start()
 
     grads = back[...]
     partial = jnp.sum(ht[...].astype(F32) * grads, axis=0, keepdims=True)
     lane = iota((peers, total_rows), 1)
-    spread = jnp.where(lax.rem(lax.div(lane, cap), peers) == iota((peers, total_rows), 0), partial, 0.0)
-    row = iota((total_rows, 128), 0)
-    place = mine * (batches * cap) + lax.div(row, peers * cap) * cap + lax.rem(row, cap)
-    gather = (iota((total_rows, 128), 1) == place).astype(F32)
-    back_rows = jnp.dot(spread, gather, precision=lax.Precision.HIGHEST, preferred_element_type=F32)
+    spread = jnp.where(((lane >> shift) & (peers - 1)) == iota((peers, total_rows), 0), partial, 0.0)
+    back_rows = jnp.dot(spread, spot[...], precision=lax.Precision.HIGHEST, preferred_element_type=F32)
     for k in range(peers):
         rs[k] = back_rows[k : k + 1, :]
     for k in range(1, peers):
@@ -252,7 +306,6 @@
 
     scaled = ((grad_scale * wrow[0:1, :]) * grads).astype(BF16)
     for batch in range(batches):
-        width = peers * cap
         dh_ref[batch] = scaled[:, batch * width : (batch + 1) * width]
 
     combine(nz - 1)
@@ -261,11 +314,15 @@
     share = zs[nz - 1]
     for step in range(nz - 1):
         share = share + zr[step]
+    dw_ref[:, :128] = grad_scale * share
+    remote(zxr, zxr, f_s, f_r, mate).wait_recv()
+    share = zx[x]
+    for k in range(nx - 1):
+        share = share + zxr[k]
     share = grad_scale * share
     depth = dw_ref.shape[0]
-    dw_ref[:, :128] = share[:depth]
-    dw_ref[: depth // 2, 128:] = share[depth:, : hidden - 128]
-    dw_ref[depth // 2 :, 128:] = share[depth:, hidden - 128 :]
+    dw_ref[: depth // 2, 128:] = share[:, : hidden - 128]
+    dw_ref[depth // 2 :, 128:] = share[:, hidden - 128 :]
 
     remote(rr, rr, ret_s, ret_r, mate).wait_recv()
     totals = rs[j]
@@ -289,6 +346,8 @@
         remote(xr.at[step], xr.at[step], x_s.at[step], x_r.at[step], mate).wait_send()
     for step in range(nz - 1):
         remote(zs.at[step], zs.at[step], z_s.at[step], z_r.at[step], mate).wait_send()
+        remote(zb.at[step], zb.at[step], b_s.at[step], b_r.at[step], mate).wait_send()
+    remote(zxr, zxr, f_s, f_r, mate).wait_send()
     remote(cxr, cxr, c_s.at[0], c_r.at[0], mate).wait_send()
     remote(czr, czr, c_s.at[1], c_r.at[1], mate).wait_send()
     remote(rr, rr, ret_s, ret_r, mate).wait_send()
@@ -303,10 +362,12 @@
     window = peers // GROUP
     cw = features // nz
     total_rows = batches * slot_count
-    piece = (features // (nz * nx)) * units // 128
+    depth = features // (nz * nx)
+    half = depth * (units - 128) // 128
     scale_top = float(batches * toks * nz * nx * peers)
     dma = pltpu.SemaphoreType.DMA
     vmem = pl.BlockSpec(memory_space=pltpu.VMEM)
+    hbm = pl.BlockSpec(memory_space=pltpu.HBM)
     dh, dw, dp = pl.pallas_call(
         functools.partial(kernel, nz, nx, scale_top),
         out_shape=(
@@ -314,9 +375,16 @@
             jax.ShapeDtypeStruct((features // (nz * nx), units), F32),
             jax.ShapeDtypeStruct((batches, choose, toks), F32),
         ),
-        in_specs=[vmem] * 4 + [pl.BlockSpec(memory_space=pltpu.SMEM)] + [vmem] * 2,
+        in_specs=[hbm] * 4 + [pl.BlockSpec(memory_space=pltpu.SMEM)] + [hbm] * 2,
         out_specs=[vmem] * 3,
         scratch_shapes=[
+            pltpu.VMEM((batches, toks, features), BF16),
+            pltpu.VMEM((batches, choose, toks), jnp.int32),
+            pltpu.VMEM((batches, choose, toks), jnp.int32),
+            pltpu.VMEM((batches, choose, toks), BF16),
+            pltpu.VMEM((units, total_rows), BF16),
+            pltpu.VMEM((units, features), BF16),
+            dma((5 + batches,)),
             pltpu.VMEM((batches, window * cap, toks), BF16),
             pltpu.VMEM((nz, window, batches, cap, cw), BF16),
             pltpu.VMEM((window, batches, cap, 128), BF16),
@@ -325,11 +393,15 @@
             pltpu.VMEM((total_rows, 128), F32),
             pltpu.VMEM((8, total_rows), F32),
             pltpu.VMEM((units, total_rows), F32),
-            pltpu.VMEM((units, total_rows), BF16),
-            pltpu.VMEM((nz, nx, piece, 128), BF16),
-            pltpu.VMEM((nz, nx - 1, piece, 128), BF16),
-            pltpu.VMEM((nz, piece, 128), F32),
-            pltpu.VMEM((nz - 1, piece, 128), F32),
+            pltpu.VMEM((total_rows, 128), F32),
+            pltpu.VMEM((nz, nx, depth, 128), BF16),
+            pltpu.VMEM((nz, nx - 1, depth, 128), BF16),
+            pltpu.VMEM((nz, depth, 128), F32),
+            pltpu.VMEM((nz - 1, depth, 128), F32),
+            pltpu.VMEM((nz, nx, half, 128), BF16),
+            pltpu.VMEM((nz - 1, nx, half, 128), BF16),
+            pltpu.VMEM((nx, half, 128), F32),
+            pltpu.VMEM((nx - 1, half, 128), F32),
             pltpu.VMEM((2, 8, 128), F32),
             pltpu.VMEM((nx - 1, 8, 128), F32),
             pltpu.VMEM((nz - 1, 8, 128), F32),
@@ -337,10 +409,10 @@
             pltpu.VMEM((peers - 1, 1, 128), F32),
             dma((nz + 1, 3)), dma((nz + 1, 3)), dma((nz + 1, 4)), dma((nz + 1, 4)),
             dma((nz + 1,)), dma((nz + 1,)), dma((nz,)), dma((nz,)),
-            dma((nz,)), dma((nz,)), dma((2,)), dma((2,)), dma, dma,
+            dma((nz,)), dma((nz,)), dma((nz,)), dma((nz,)), dma, dma, dma((2,)), dma((2,)), dma, dma,
         ],
         compiler_params=pltpu.CompilerParams(
-            collective_id=0, has_side_effects=True, vmem_limit_bytes=32 * 1024 * 1024
+            collective_id=0, has_side_effects=True, vmem_limit_bytes=60 * 1024 * 1024
         ),
     )(
         d_out,

time: 77.6 us -> 63.7 us (0.82)
  Pallas kernels: 69.3 us -> 59.9 us
  local copies, waits for them, and re-layouts: 7.24 us -> 2.93 us
    pallas_call x1, Pallas kernels: 69.3 us -> 59.9 us  [on_device(): pl.pallas_call(functools.partial(kernel, nz, nx, scale_top), out_shape=(j...]
    unnamed x17 -> x7, local copies, waits for them, and re-layouts: 7.24 us -> 2.93 us
where the time goes in v2:
time: 63.7 us; the launch traced here: 63.5 us
  Pallas kernels  59.9 us (94%)
  local copies, waits for them, and re-layouts  2.93 us (5%)
  between operations  0.65 us (1%)
    pallas_call x1, Pallas kernels, on_device(): pl.pallas_call(functools.partial(kernel, nz, nx, scale_top), out_shape=(j...  59.9 us
    unnamed x7, local copies, waits for them, and re-layouts  2.93 us

profile of v2, /device:TPU:1, one launch (start us, length us, event | category | flops | bytes accessed | tf_op | source)
XLA Modules:
  0.0 63.5 jit_solution(16638353776377214408)
XLA Ops:
  0.6 59.9 %shard_map.94 = (bf16[2,192,256]{2,1,0:T(8,128)(2,1)}, f32[32,192]{1,0:T(8,128)}, f32[2,8,128]{2,1,0:T(8,128)}) custom-call(bf16[2,128,2048]{2,1,0:T(8,128)(2,1)} %dout_hbm.1, s32[2,8,128]{2,1,0:T(8,128)} %bitcast.15, s32[2,8,128]{2,1,0:T(8,128)} %bitcast.16, bf16[2,8,128]{2,1,0:T(8,128)(2,1)} %bitcast.18, s32[1,2]{1,0:T(1,128)} %bitcast.19, ...), custom_call_target="tpu_custom_call" | custom-call | tf_op jit(solution)/shard_map/pallas_call | solution.py:371
  60.5 0.0 copy-start
  60.5 1.6 %copy.14 = bf16[2,1,256,192]{2,3,1,0:T(8,128)(2,1)} copy(bf16[2,1,256,192]{2,3,1,0:T(8,128)(2,1)} %bitcast.14) | data formatting | bytes 393216
  62.1 0.0 copy-done
  62.1 0.0 copy-start.1
  62.1 0.6 copy.15
  62.8 0.1 copy-done.1
  62.9 0.6 copy.16
Async XLA Ops:
  60.5 1.6 %copy-start = (f32[32,192]{1,0:T(8,128)S(1)}, f32[32,192]{1,0:T(8,128)}, u32[]{:S(2)}) copy-start(f32[32,192]{1,0:T(8,128)} %get-tuple-element.16) | copy-start | bytes 73732
  62.1 0.7 %copy-start.1 = (f32[2,8,128]{2,1,0:T(8,128)S(1)}, f32[2,8,128]{2,1,0:T(8,128)}, u32[]{:S(2)}) copy-start(f32[2,8,128]{2,1,0:T(8,128)} %get-tuple-element.8) | copy-start | bytes 24580

commit v3 on v2

--- a/solution.py
+++ b/solution.py
@@ -277,17 +277,7 @@
 
         return carry
 
-    lax.fori_loop(0, nz + max(MATE_LAG + SIB_LAG, MATE_LAG + SIB_LAG + SUM_LAG - 1), body, 0)
-
-    for step in range(nz - 1):
-        remote(zbr.at[step], zbr.at[step], b_s.at[step], b_r.at[step], mate).wait_recv()
-    block = zb[nz - 1].astype(F32)
-    for step in range(nz - 1):
-        block = block + zbr[step].astype(F32)
-    zx[...] = block
-    for k in range(1, nx):
-        there = lax.rem(x + k, nx)
-        remote(zx.at[there], zxr.at[k - 1], f_s, f_r, (z * nx + there, j)).start()
+    lax.fori_loop(0, nz + MATE_LAG + SIB_LAG, body, 0)
 
     grads = back[...]
     partial = jnp.sum(ht[...].astype(F32) * grads, axis=0, keepdims=True)
@@ -299,6 +289,23 @@
     for k in range(1, peers):
         there = lax.rem(j + k, peers)
         remote(rs.at[there], rr.at[k - 1], ret_s, ret_r, (d, there)).start()
+
+    for step in range(nz - 1):
+        remote(zbr.at[step], zbr.at[step], b_s.at[step], b_r.at[step], mate).wait_recv()
+    block = zb[nz - 1].astype(F32)
+    for step in range(nz - 1):
+        block = block + zbr[step].astype(F32)
+    zx[...] = block
+    for k in range(1, nx):
+        there = lax.rem(x + k, nx)
+        remote(zx.at[there], zxr.at[k - 1], f_s, f_r, (z * nx + there, j)).start()
+
+    def rest(step, carry):
+        combine(step)
+        send_z(step)
+        return carry
+
+    lax.fori_loop(max(nz - SUM_LAG, 0), nz - 1, rest, 0)
 
     remote(czr, czr, c_s.at[1], c_r.at[1], mate).wait_recv()
     token_total = jnp.sum((cs[1] + jnp.sum(czr[...], axis=0))[0:1, 0:1], axis=0, keepdims=True)

time: 63.7 us -> 60.5 us (0.950)
  Pallas kernels: 59.9 us -> 56.7 us
    pallas_call x1, Pallas kernels: 59.9 us -> 56.7 us  [on_device(): pl.pallas_call(functools.partial(kernel, nz, nx, scale_top), out_shape=(j...]
where the time goes in v3:
time: 60.5 us; the launch traced here: 60.3 us
  Pallas kernels  56.7 us (94%)
  local copies, waits for them, and re-layouts  2.93 us (5%)
  between operations  0.65 us (1%)
    pallas_call x1, Pallas kernels, on_device(): pl.pallas_call(functools.partial(kernel, nz, nx, scale_top), out_shape=(j...  56.7 us
    unnamed x7, local copies, waits for them, and re-layouts  2.93 us

profile of v3, /device:TPU:1, one launch (start us, length us, event | category | flops | bytes accessed | tf_op | source)
XLA Modules:
  0.0 60.3 jit_solution(8602290594187536666)
XLA Ops:
  0.6 56.7 %shard_map.94 = (bf16[2,192,256]{2,1,0:T(8,128)(2,1)}, f32[32,192]{1,0:T(8,128)}, f32[2,8,128]{2,1,0:T(8,128)}) custom-call(bf16[2,128,2048]{2,1,0:T(8,128)(2,1)} %dout_hbm.1, s32[2,8,128]{2,1,0:T(8,128)} %bitcast.15, s32[2,8,128]{2,1,0:T(8,128)} %bitcast.16, bf16[2,8,128]{2,1,0:T(8,128)(2,1)} %bitcast.18, s32[1,2]{1,0:T(1,128)} %bitcast.19, ...), custom_call_target="tpu_custom_call" | custom-call | tf_op jit(solution)/shard_map/pallas_call | solution.py:378
  57.4 0.0 copy-start
  57.4 1.6 %copy.14 = bf16[2,1,256,192]{2,3,1,0:T(8,128)(2,1)} copy(bf16[2,1,256,192]{2,3,1,0:T(8,128)(2,1)} %bitcast.14) | data formatting | bytes 393216
  59.0 0.0 copy-done
  59.0 0.0 copy-start.1
  59.0 0.6 %copy.15 = f32[32,192]{1,0:T(8,128)} copy(f32[32,192]{1,0:T(8,128)S(1)} %copy-done) | data formatting | bytes 49152
  59.6 0.1 copy-done.1
  59.7 0.6 copy.16
Async XLA Ops:
  57.4 1.6 %copy-start = (f32[32,192]{1,0:T(8,128)S(1)}, f32[32,192]{1,0:T(8,128)}, u32[]{:S(2)}) copy-start(f32[32,192]{1,0:T(8,128)} %get-tuple-element.16) | copy-start | bytes 73732
  59.0 0.7 %copy-start.1 = (f32[2,8,128]{2,1,0:T(8,128)S(1)}, f32[2,8,128]{2,1,0:T(8,128)}, u32[]{:S(2)}) copy-start(f32[2,8,128]{2,1,0:T(8,128)} %get-tuple-element.8) | copy-start | bytes 24580
